TPU v7x, 32 devices: a whole 2x2x4 slice. The times are simulated.
32 devices in a mesh: grp: 2 (over core), dp: 16 (over z, y, x).
Axes of the slice: x: 2, y: 2, z: 4, core: 2. Of those that a mesh axis runs over, the one named last changes fastest.
Arguments:
- tokens: bfloat16 [32768, 768], P(('grp', 'dp')), may hold values from -6 to 6
- out_grad: bfloat16 [32768, 768], P(('grp', 'dp')), may hold values from -6 to 6
- image_counts: int32 [32, 32], P(('grp', 'dp')), may hold values from 0 to 98, as said below
- group_of_device: int32 [32], P(('grp', 'dp')), may hold values from 0 to 2, as said below
- group_weight: int32 [3], replicated, may hold values from 1 to 4
- norm1_gain: bfloat16 [768], replicated, may hold values from 0.5 to 1.5
- norm1_bias: bfloat16 [768], replicated, may hold values from -4 to 4
- qkv_weight: bfloat16 [768, 2304], replicated, may hold values from -0.21875 to 0.21875
- qkv_bias: bfloat16 [2304], replicated, may hold values from -4 to 4
- proj_weight: bfloat16 [768, 768], replicated, may hold values from -0.875 to 0.875
- proj_bias: bfloat16 [768], replicated, may hold values from -4 to 4
- norm2_gain: bfloat16 [768], replicated, may hold values from 0.5 to 1.5
- norm2_bias: bfloat16 [768], replicated, may hold values from -4 to 4
- fc1_weight: bfloat16 [768, 3072], replicated, may hold values from -0.21875 to 0.21875
- fc1_bias: bfloat16 [3072], replicated, may hold values from -4 to 4
- fc2_weight: bfloat16 [3072, 768], replicated, may hold values from -0.109375 to 0.109375
- fc2_bias: bfloat16 [768], replicated, may hold values from -4 to 4
- first_moment: float32 [16, 442992], P('dp'), may hold values from -2.5 to 2.5
- second_moment: float32 [16, 442992], P('dp'), may hold values from 1e-05 to 0.001
Outputs:
- block_out: bfloat16 [32768, 768], P(('grp', 'dp'))
- input_grad: bfloat16 [32768, 768], P(('grp', 'dp'))
- weight_grads: float32 [16, 442992], P('dp')
- new_weights: bfloat16 [16, 442992], replicated
- new_first: float32 [16, 442992], P('dp')
- new_second: float32 [16, 442992], P('dp')
- fc2_bias_grad: float32 [768], P('dp')
Inputs may be any that keep to these rules, and one draw needn't show every extreme that they name: `group_of_device`: each of the 3 groups holds some devices: about a half, a third and a sixth of them. `image_counts`: in each device's row the live images come first, at least one, each with 30 to 98 visible patches, summing to at most 1024; the remaining slots are 0.
All inputs are finite; a program needn't handle non-finite values.
Results may differ from a plain program's by a relative error of at most 0.012.
Values may be sent and summed in bfloat16 or wider, within the bound.
No kernel may reach another device: no remote copies, remote signals or barrier semaphores. Data moves between devices by JAX's collectives and lax.ppermute only.
A program may use at most 320 MiB of HBM per device.

v0:
```python
import jax
import jax.numpy as jnp
from jax import lax
from jax.sharding import PartitionSpec as P

D = 768
HEADS = 12
HEAD_DIM = 64
NGROUPS = 3
beta_one = 0.9
beta_two = 0.999
adam_eps = 1e-08
decay_rate = 0.05
step_count = 10.0
learn_rate = 0.004 * 0.75**1
norm_eps = 1e-06
neg_fill = -1e30
decay_flags = (0.0, 0.0, 1.0, 0.0, 1.0, 0.0, 0.0, 0.0, 1.0, 0.0, 1.0, 0.0)


def layer_norm(values, gain, shift):
    center = values - jnp.mean(values, axis=-1, keepdims=True)
    spread = jnp.mean(center * center, axis=-1, keepdims=True)
    return center * lax.rsqrt(spread + norm_eps) * gain + shift


def gelu_tanh(values):
    return jax.nn.gelu(values, approximate=True)


def contract_rows(first_op, second_op):
    return lax.dot_general(
        first_op, second_op, (((0,), (0,)), ((), ())), preferred_element_type=jnp.float32
    )


def contract_cols(first_op, second_op):
    return lax.dot_general(
        first_op, second_op, (((1,), (1,)), ((), ())), preferred_element_type=jnp.float32
    )


def segment_info(counts_row, length):
    segment_ends = jnp.cumsum(counts_row)
    position = lax.iota(jnp.int32, length)
    segment = jnp.sum((position[:, None] >= segment_ends[None, :]).astype(jnp.int32), axis=1)
    return (segment, position < segment_ends[-1])


def score_block(query_part, key_rows, same_segment):
    raw = (
        jnp.einsum("qhd,khd->hqk", query_part, key_rows, preferred_element_type=jnp.float32) * 0.125
    )
    return jnp.where(same_segment[None], raw, neg_fill)


def on_device(
    tokens,
    out_grad,
    image_counts,
    group_of_device,
    group_weight,
    norm1_gain,
    norm1_bias,
    qkv_weight,
    qkv_bias,
    proj_weight,
    proj_bias,
    norm2_gain,
    norm2_bias,
    fc1_weight,
    fc1_bias,
    fc2_weight,
    fc2_bias,
    first_moment,
    second_moment,
):
    length = tokens.shape[0]
    segment, valid_rows = segment_info(image_counts[0], length)
    images = jnp.sum((image_counts[0] > 0).astype(jnp.int32))
    member = (group_of_device[0] == lax.iota(jnp.int32, NGROUPS)).astype(jnp.int32)
    totals = lax.psum(member * images, ("grp", "dp"))
    factor = jnp.sum(member * group_weight).astype(jnp.float32) / jnp.sum(member * totals).astype(
        jnp.float32
    )
    inputs = tokens.astype(jnp.float32)
    normed_one, norm_one_back = jax.vjp(
        layer_norm, inputs, norm1_gain.astype(jnp.float32), norm1_bias.astype(jnp.float32)
    )
    normed_one_low = normed_one.astype(jnp.bfloat16)
    projected = (
        jnp.dot(normed_one_low, qkv_weight, preferred_element_type=jnp.float32)
        + qkv_bias.astype(jnp.float32)
    ).astype(jnp.bfloat16)
    query_rows = projected[:, :D].reshape(length, HEADS, HEAD_DIM)
    key_rows = projected[:, D : 2 * D].reshape(length, HEADS, HEAD_DIM)
    value_rows = projected[:, 2 * D :].reshape(length, HEADS, HEAD_DIM)
    block_rows = min(512, length)
    offsets = list(range(0, length, block_rows))
    context_parts = []
    log_sums = []
    for offset in offsets:
        same_segment = segment[offset : offset + block_rows, None] == segment[None, :]
        scores = score_block(query_rows[offset : offset + block_rows], key_rows, same_segment)
        row_max = jnp.max(scores, axis=-1, keepdims=True)
        exponent = jnp.exp(scores - row_max)
        row_sum = jnp.sum(exponent, axis=-1, keepdims=True)
        attn_probs = exponent / row_sum
        log_sums.append(row_max + jnp.log(row_sum))
        context_parts.append(
            jnp.einsum(
                "hqk,khd->qhd",
                attn_probs.astype(jnp.bfloat16),
                value_rows,
                preferred_element_type=jnp.float32,
            )
        )
    context = jnp.concatenate(context_parts, axis=0).reshape(length, D).astype(jnp.bfloat16)
    middle = inputs + (
        jnp.dot(context, proj_weight, preferred_element_type=jnp.float32)
        + proj_bias.astype(jnp.float32)
    )
    normed_two, norm_two_back = jax.vjp(
        layer_norm, middle, norm2_gain.astype(jnp.float32), norm2_bias.astype(jnp.float32)
    )
    normed_two_low = normed_two.astype(jnp.bfloat16)
    hidden = jnp.dot(
        normed_two_low, fc1_weight, preferred_element_type=jnp.float32
    ) + fc1_bias.astype(jnp.float32)
    activated, gelu_back = jax.vjp(gelu_tanh, hidden)
    activated_low = activated.astype(jnp.bfloat16)
    block_out = (
        middle
        + (
            jnp.dot(activated_low, fc2_weight, preferred_element_type=jnp.float32)
            + fc2_bias.astype(jnp.float32)
        )
    ).astype(jnp.bfloat16)
    grad_out = out_grad.astype(jnp.float32) * valid_rows[:, None].astype(jnp.float32)
    grad_out_low = grad_out.astype(jnp.bfloat16)
    fc2_grad = contract_rows(activated_low, grad_out_low)
    fc2_bias_grad = jnp.sum(grad_out, axis=0)
    grad_hidden = gelu_back(contract_cols(grad_out_low, fc2_weight))[0].astype(jnp.bfloat16)
    fc1_grad = contract_rows(normed_two_low, grad_hidden)
    fc1_bias_grad = jnp.sum(grad_hidden.astype(jnp.float32), axis=0)
    grad_middle_norm, gain_two_grad, shift_two_grad = norm_two_back(
        contract_cols(grad_hidden, fc1_weight)
    )
    grad_middle = grad_out + grad_middle_norm
    grad_branch = grad_middle.astype(jnp.bfloat16)
    proj_grad = contract_rows(context, grad_branch)
    proj_bias_grad = jnp.sum(grad_branch.astype(jnp.float32), axis=0)
    grad_context = (
        contract_cols(grad_branch, proj_weight)
        .astype(jnp.bfloat16)
        .reshape(length, HEADS, HEAD_DIM)
    )
    grad_keys = jnp.zeros((length, HEADS, HEAD_DIM), jnp.float32)
    grad_values = jnp.zeros((length, HEADS, HEAD_DIM), jnp.float32)
    query_grads = []
    for piece_index, offset in enumerate(offsets):
        query_part = query_rows[offset : offset + block_rows]
        context_grad_part = grad_context[offset : offset + block_rows]
        same_segment = segment[offset : offset + block_rows, None] == segment[None, :]
        attn_probs = jnp.exp(
            score_block(query_part, key_rows, same_segment) - log_sums[piece_index]
        )
        grad_probs = jnp.einsum(
            "qhd,khd->hqk", context_grad_part, value_rows, preferred_element_type=jnp.float32
        )
        grad_scores = (
            attn_probs * (grad_probs - jnp.sum(attn_probs * grad_probs, axis=-1, keepdims=True))
        ).astype(jnp.bfloat16)
        query_grads.append(
            jnp.einsum("hqk,khd->qhd", grad_scores, key_rows, preferred_element_type=jnp.float32)
            * 0.125
        )
        grad_keys = (
            grad_keys
            + jnp.einsum(
                "hqk,qhd->khd", grad_scores, query_part, preferred_element_type=jnp.float32
            )
            * 0.125
        )
        grad_values = grad_values + jnp.einsum(
            "hqk,qhd->khd",
            attn_probs.astype(jnp.bfloat16),
            context_grad_part,
            preferred_element_type=jnp.float32,
        )
    grad_projected = jnp.concatenate(
        [
            jnp.concatenate(query_grads, axis=0).reshape(length, D),
            grad_keys.reshape(length, D),
            grad_values.reshape(length, D),
        ],
        axis=1,
    ).astype(jnp.bfloat16)
    qkv_grad = contract_rows(normed_one_low, grad_projected)
    qkv_bias_grad = jnp.sum(grad_projected.astype(jnp.float32), axis=0)
    grad_input_norm, gain_one_grad, shift_one_grad = norm_one_back(
        contract_cols(grad_projected, qkv_weight)
    )
    input_grad = (grad_middle + grad_input_norm).astype(jnp.bfloat16)
    row_count = lax.axis_size("dp")
    grad_list = (
        gain_one_grad,
        shift_one_grad,
        qkv_grad,
        qkv_bias_grad,
        proj_grad,
        proj_bias_grad,
        gain_two_grad,
        shift_two_grad,
        fc1_grad,
        fc1_bias_grad,
        fc2_grad,
        fc2_bias_grad,
    )
    packed = jnp.concatenate(
        [(grad_item * factor).reshape(row_count, -1) for grad_item in grad_list], axis=1
    )
    grad_part = lax.psum_scatter(packed, "dp", scatter_dimension=0, tiled=True)
    summed = lax.psum(grad_part, "grp")
    bias_width = fc2_bias.shape[0] // row_count
    summed_bias = summed[0, summed.shape[1] - bias_width :]
    own_index = lax.axis_index("dp")
    weight_list = (
        norm1_gain,
        norm1_bias,
        qkv_weight,
        qkv_bias,
        proj_weight,
        proj_bias,
        norm2_gain,
        norm2_bias,
        fc1_weight,
        fc1_bias,
        fc2_weight,
        fc2_bias,
    )
    current = jnp.concatenate(
        [
            lax.dynamic_slice_in_dim(weight_item.reshape(row_count, -1), own_index, 1, 0).astype(
                jnp.float32
            )
            for weight_item in weight_list
        ],
        axis=1,
    )
    decay = jnp.concatenate(
        [
            jnp.full((1, weight_item.size // row_count), decay_flag, jnp.float32)
            for weight_item, decay_flag in zip(weight_list, decay_flags)
        ],
        axis=1,
    )
    new_first = beta_one * first_moment + (1.0 - beta_one) * summed
    new_second = beta_two * second_moment + (1.0 - beta_two) * summed * summed
    ratio = (
        new_first
        / (1.0 - beta_one**step_count)
        / (jnp.sqrt(new_second / (1.0 - beta_two**step_count)) + adam_eps)
    )
    fresh_low = (current - learn_rate * (ratio + decay_rate * decay * current)).astype(jnp.bfloat16)
    new_weights = lax.all_gather(fresh_low, "dp", axis=0, tiled=True)
    return (block_out, input_grad, summed, new_weights, new_first, new_second, summed_bias)


def solution(mesh):
    in_specs = (
        P(("grp", "dp"), None),
        P(("grp", "dp"), None),
        P(("grp", "dp"), None),
        P(("grp", "dp")),
        P(),
        P(),
        P(),
        P(),
        P(),
        P(),
        P(),
        P(),
        P(),
        P(),
        P(),
        P(),
        P(),
        P("dp", None),
        P("dp", None),
    )
    out_specs = (
        P(("grp", "dp"), None),
        P(("grp", "dp"), None),
        P("dp", None),
        P(),
        P("dp", None),
        P("dp", None),
        P("dp"),
    )
    return jax.shard_map(
        on_device, mesh=mesh, in_specs=in_specs, out_specs=out_specs, check_vma=False
    )
```

profile of v0, /device:TPU:0, one launch (start us, length us, event | category | flops | bytes accessed | tf_op | source)
XLA Modules:
  0.0 1624.3 jit_solution(11156478044281256966)
XLA Ops:
  10.4 6.4 add_convert_fusion
  26.9 12.2 fusion.19
  39.1 11.8 fusion
  54.0 12.7 fusion.44
  69.0 12.4 fusion.20
  81.4 13.4 fusion.1
  97.3 8.5 fusion.45
  114.6 10.8 fusion.63
  125.5 16.4 %convert_reduce_fusion = (f32[3072]{0:T(1024)}, bf16[1024,3072]{1,0:T(8,128)(2,1)S(1)}) fusion(f32[1024,3072]{1,0:T(8,128)} %fusion.63, f32[3072]{0:T(1024)S(1)} %convert_element_type.143, bf16[3072,768]{1,0:T(8,128)(2,1)} %param.34, bf16[1024,768]{0,1:T(8,128)(2,1)S(1)} %copy-done.14, f32[1024]{0:T(1024)S(1)} %fusion.47), kind=kOutput, calls=%fused_computation.28 | convolution fusion | flops 4906546176 | bytes 25194496 | tf_op jit(solution)/shard_map/dot_general | solution.py:38
  141.9 7.3 fusion.73
  149.2 3.5 copy.98
  162.8 21.6 %multiply_reduce_fusion.1 = (f32[12,512]{1,0:T(8,128)S(1)}, f32[12,512,1024]{2,1,0:T(8,128)}) fusion(f32[12,512]{1,0:T(8,128)S(1)} %copy-done.43, f32[12,512,1024]{2,1,0:T(8,128)} %get-tuple-element.68, pred[512,1024]{1,0:T(8,128)(4,1)S(1)} %copy-done.18, bf16[512,12,64]{0,2,1:T(8,128)(2,1)S(1)} %bitcast.95, bf16[1024,12,64]{0,2,1:T(8,128)(2,1)S(1)} %bitcast.81), kind=kOutput, calls=%fused_computation.4 | convolution fusion | flops 836757504 | bytes 53264384 | tf_op jit(solution)/shard_map/qhd,khd->hqk/dot_general | solution.py:168
  184.4 17.7 %multiply_reduce_fusion = (f32[12,512]{1,0:T(8,128)S(1)}, f32[12,512,1024]{2,1,0:T(8,128)}) fusion(f32[12,512]{1,0:T(8,128)S(1)} %log_add_fusion, f32[12,512,1024]{2,1,0:T(8,128)} %get-tuple-element.66, pred[512,1024]{1,0:T(8,128)(4,1)S(1)} %copy-done.20, bf16[512,12,64]{0,2,1:T(8,128)(2,1)} %bitcast.97, bf16[1024,12,64]{0,2,1:T(8,128)(2,1)S(1)} %bitcast.82), kind=kOutput, calls=%fused_computation.1 | convolution fusion | flops 836757504 | bytes 53264384 | tf_op jit(solution)/shard_map/qhd,khd->hqk/dot_general | solution.py:168
  202.1 42.2 %multiply_convert_fusion = (bf16[12,512,1024]{2,1,0:T(8,128)(2,1)}, bf16[12,512,1024]{2,1,0:T(8,128)(2,1)}) fusion(f32[12,512,1024]{2,1,0:T(8,128)} %get-tuple-element.74, f32[12,512]{1,0:T(8,128)S(1)} %get-tuple-element.73, f32[12,512]{1,0:T(8,128)S(1)} %log_add_fusion, f32[12,512,1024]{2,1,0:T(8,128)} %get-tuple-element.66, ...), kind=kLoop, calls=%fused_computation | loop fusion | flops 75497472 | bytes 126976000 | tf_op jit(solution)/shard_map/convert_element_type | solution.py:173
  244.3 9.6 fusion.42
  253.9 8.8 fusion.74
  262.7 13.3 fusion.11
  276.7 6.3 fusion.43
  283.0 5.6 multiply_convert_fusion.3
  288.6 13.0 add_convert_fusion.2
  305.3 5.6 fusion.72
  312.1 42.2 %psum.14 = s32[3]{0:T(128)S(1)} all-reduce(s32[3]{0:T(128)S(1)} %fusion.51), channel_id=1, replica_groups=mesh['grp'=2,'dp'=16] {'grp','dp'}, use_global_device_ids=true, to_apply=%region_19.20 | all-reduce | flops 3 | bytes 24 | tf_op jit(solution)/shard_map/psum | solution.py:82
  357.0 9.0 convolution_multiply_fusion
  368.9 10.7 convolution_multiply_fusion.2
  379.7 10.9 convolution_multiply_fusion.1
  390.7 5.6 reshape.518
  396.3 4.0 copy.99
  407.8 10.7 reshape.520
  418.6 10.6 reshape.521
  429.2 5.6 fusion.32
  437.7 20.7 %dynamic-update-slice.24 = f32[16,442992]{1,0:T(8,128)} dynamic-update-slice(f32[16,442992]{1,0:T(8,128)} %dynamic-update-slice.23, f32[16,110592]{1,0:T(8,128)} %reshape.518, s32[]{} %constant.87, s32[]{} %constant.88) | dynamic-update-slice | bytes 14155780
  459.9 7.6 dynamic-update-slice.26
  471.9 6.5 constant_dynamic-update-slice_fusion
  479.8 27.0 %dynamic-update-slice.32 = f32[16,442992]{1,0:T(8,128)} dynamic-update-slice(f32[16,442992]{1,0:T(8,128)} %dynamic-update-slice.31, f32[16,147456]{1,0:T(8,128)} %reshape.521, s32[]{} %constant.87, s32[]{} %constant.95) | dynamic-update-slice | bytes 18874372
  518.2 5.2 reshape.530
  523.4 5.2 reshape.532
  533.8 8.7 dynamic-update-slice.1
  544.0 3.8 dynamic-update-slice.3
  555.0 8.8 dynamic-update-slice.12
  565.3 3.7 dynamic-update-slice.14
  576.1 667.0 %all-reduce.6.cloned.1.call-done = f32[16,442992]{1,0:T(8,128)} async-done(((f32[16,442992]{1,0:T(8,128)}), f32[16,442992]{1,0:T(8,128)}) %all-reduce.6.cloned.1.call-update) | async-done | bytes 28351504
  1243.1 7.5 constant_dynamic-slice_fusion.11
  1255.6 11.4 dynamic-update-slice.8
  1269.6 11.3 dynamic-update-slice.20
  1282.1 14.6 convert_bitcast_fusion
  1299.5 11.8 add_convert_fusion.3
  1315.2 282.6 %all-gather.3.cloned.1.call-done = bf16[16,1,442992]{2,1,0:T(2,128)(2,1)} async-done(((bf16[1,1,442992]{2,1,0:T(2,128)(2,1)}), bf16[16,1,442992]{2,1,0:T(2,128)(2,1)}) %all-gather.3.cloned.1.call-update) | async-done | bytes 14175760 | tf_op jit(solution)/shard_map/all_gather | solution.py:266
  1597.8 18.5 %copy.107 = bf16[16,1,442992]{2,0,1:T(8,128)(2,1)} copy(bf16[16,1,442992]{2,1,0:T(2,128)(2,1)} %all-gather.3.cloned.1.call-done) | data formatting | bytes 28351488
  (313 shorter events, 116.6 us)
Async XLA Ops:
  7.2 1235.9 %all-reduce.6.cloned.1.call-start = ((), (), s32[]{:S(2)}) async-start(), calls=%async_computation.2 | async-start | bytes 56705024
  9.0 98.3 %copy-start.1 = (bf16[1024,768]{0,1:T(8,128)(2,1)}, bf16[1024,768]{0,1:T(8,128)(2,1)S(1)}, u32[]{:S(2)}) copy-start(bf16[1024,768]{0,1:T(8,128)(2,1)S(1)} %copy.90) | copy-start | bytes 4718596
  22.5 46.6 %copy-start.8 = (bf16[1024,768]{0,1:T(8,128)(2,1)}, bf16[1024,768]{0,1:T(8,128)(2,1)S(1)}, u32[]{:S(2)}) copy-start(bf16[1024,768]{0,1:T(8,128)(2,1)S(1)} %copy.94) | copy-start | bytes 4718596
  26.9 12.2 copy-start.17
  69.0 25.9 %copy-start.12 = (bf16[1024,768]{0,1:T(8,128)(2,1)S(1)}, bf16[1024,768]{0,1:T(8,128)(2,1)}, u32[]{:S(2)}) copy-start(bf16[1024,768]{0,1:T(8,128)(2,1)} %copy.91) | copy-start | bytes 4718596
  81.4 15.8 copy-start
  81.4 15.9 copy-start.19
  97.3 8.5 copy-start.40
  111.1 14.4 copy-start.41
  114.6 10.9 copy-start.60
  114.6 10.9 copy-start.14
  114.6 27.3 %slice-start.3 = ((s8[4718592]{0:T(1024)(128)(4,1)}), s8[4194304]{0:T(1024)(128)(4,1)S(1)}, s32[]{:S(2)}) async-start(s8[4718592]{0:T(1024)(128)(4,1)} %bitcast.76), calls=%async_computation.6 | async-start | bytes 8388608
  125.5 16.4 %slice-start.4 = ((s8[4718592]{0:T(1024)(128)(4,1)}), s8[524288]{0:T(1024)(128)(4,1)S(1)}, s32[]{:S(2)}) async-start(s8[4718592]{0:T(1024)(128)(4,1)} %bitcast.76), calls=%async_computation.7 | async-start | bytes 1048576
  162.0 22.4 %copy-start.30 = (bf16[512,768]{0,1:T(8,128)(2,1)}, bf16[512,768]{0,1:T(8,128)(2,1)S(1)}, u32[]{:S(2)}) copy-start(bf16[512,768]{0,1:T(8,128)(2,1)S(1)} %get-tuple-element.59) | copy-start | bytes 2359300
  162.8 21.7 %copy-start.20 = (pred[512,1024]{1,0:T(8,128)(4,1)S(1)}, pred[512,1024]{1,0:T(8,128)(4,1)}, u32[]{:S(2)}) copy-start(pred[512,1024]{1,0:T(8,128)(4,1)} %get-tuple-element.62) | copy-start | bytes 1572868
  202.1 42.2 %copy-start.9 = (bf16[1024,768]{0,1:T(8,128)(2,1)S(1)}, bf16[1024,768]{0,1:T(8,128)(2,1)}, u32[]{:S(2)}) copy-start(bf16[1024,768]{0,1:T(8,128)(2,1)} %copy-done.8) | copy-start | bytes 4718596
  244.3 9.6 copy-start.24
  253.9 8.8 copy-start.21
  253.9 8.8 copy-start.31
  253.9 22.7 %slice-start = ((s8[12582912]{0:T(1024)(128)(4,1)}), s8[4194304]{0:T(1024)(128)(4,1)S(1)}, s32[]{:S(2)}) async-start(s8[12582912]{0:T(1024)(128)(4,1)} %bitcast.70), calls=%async_computation.3 | async-start | bytes 8388608
  253.9 22.7 %slice-start.1 = ((s8[12582912]{0:T(1024)(128)(4,1)}), s8[4194304]{0:T(1024)(128)(4,1)S(1)}, s32[]{:S(2)}) async-start(s8[12582912]{0:T(1024)(128)(4,1)} %bitcast.70), calls=%async_computation.4 | async-start | bytes 8388608
  262.7 13.3 copy-start.77
  262.7 13.9 slice-start.2
  288.6 13.1 copy-start.28
  288.6 13.1 copy-start.29
  301.8 9.0 copy-start.26
  305.3 50.3 %copy-start.78 = (s32[3]{0:T(128)S(1)}, s32[3]{0:T(128)}, u32[]{:S(2)}) copy-start(s32[3]{0:T(128)} %param.23) | copy-start | bytes 40
  305.3 51.7 %copy-start.2 = (bf16[1024,768]{0,1:T(8,128)(2,1)S(1)}, bf16[1024,768]{0,1:T(8,128)(2,1)}, u32[]{:S(2)}) copy-start(bf16[1024,768]{0,1:T(8,128)(2,1)} %copy-done.1) | copy-start | bytes 4718596
  305.3 51.7 %copy-start.45 = (f32[1024]{0:T(1024)S(1)}, f32[1024]{0:T(1024)}, u32[]{:S(2)}) copy-start(f32[1024]{0:T(1024)} %copy-done.44) | copy-start | bytes 12292
  305.3 51.7 %copy-start.47 = (f32[768]{0:T(1024)S(1)}, f32[768]{0:T(1024)}, u32[]{:S(2)}) copy-start(f32[768]{0:T(1024)} %copy-done.46) | copy-start | bytes 9220
  305.3 51.7 %copy-start.49 = (f32[1024]{0:T(1024)S(1)}, f32[1024]{0:T(1024)}, u32[]{:S(2)}) copy-start(f32[1024]{0:T(1024)} %copy-done.48) | copy-start | bytes 12292
  305.3 51.7 %copy-start.74 = (f32[768]{0:T(1024)S(1)}, f32[768]{0:T(1024)}, u32[]{:S(2)}) copy-start(f32[768]{0:T(1024)} %copy-done.73) | copy-start | bytes 9220
  357.0 9.0 copy-start.34
  357.0 9.0 copy-start.36
  366.0 13.7 slice-start.5
  368.9 10.8 copy-start.16
  368.9 10.8 slice-start.6
  368.9 10.8 slice-start.7
  368.9 10.8 copy-start.61
  407.8 10.7 copy-start.63
  418.6 10.7 copy-start.53
  437.7 22.2 %copy-start.23 = (f32[16,36864]{1,0:T(8,128)S(1)}, f32[16,36864]{1,0:T(8,128)}, u32[]{:S(2)}) copy-start(f32[16,36864]{1,0:T(8,128)} %reshape.519) | copy-start | bytes 7077892
  508.1 774.0 %all-reduce.4.cloned.1.call-start = ((), (), s32[]{:S(2)}) async-start(), calls=%async_computation | async-start | bytes 3544064 | tf_op jit(solution)/shard_map/psum | solution.py:224
  1243.1 10.7 copy-start.57
  1243.1 10.7 copy-start.72
  1250.7 31.4 %copy-start.32 = (f32[1,442992]{1,0:T(1,128)S(1)}, f32[1,442992]{1,0:T(1,128)}, u32[]{:S(2)}) copy-start(f32[1,442992]{1,0:T(1,128)} %param.36) | copy-start | bytes 5315908
  1250.7 347.1 %all-gather.3.cloned.1.call-start = ((), (), s32[]{:S(2)}) async-start(), calls=%async_computation.1 | async-start | bytes 30124544 | tf_op jit(solution)/shard_map/all_gather | solution.py:266
  1315.2 301.2 %copy-start.25 = (f32[1,442992]{1,0:T(1,128)S(1)}, f32[1,442992]{1,0:T(1,128)}, u32[]{:S(2)}) copy-start(f32[1,442992]{1,0:T(1,128)} %all-reduce.4.cloned.1.call-done) | copy-start | bytes 5315908
  (43 other events, 131.1 us)
Sparse Core Ops, SparseCore 0:
  508.2 734.8 all-reduce.5
  1250.8 19.8 all-reduce.3
  1296.9 300.8 all-gather.2
where the time goes:
time: 1640 us; the launch traced here: 1620 us
  waiting for transfers between devices  950 us (58%)
  local copies, waits for them, and re-layouts  272 us (17%)
  matrix products  237 us (14%)
  other arithmetic  106 us (6%)
  blocking collectives  42.2 us (3%)
  between operations  17 us (1%)
    unnamed x4, waiting for transfers between devices  667 us
    all_gather x1, waiting for transfers between devices, on_device(): new_weights = lax.all_gather(fresh_low, 'dp', axis=0, tiled=True)  283 us
    unnamed x215, local copies, waits for them, and re-layouts  188 us
    psum x1, blocking collectives, on_device(): totals = lax.psum(member * images, ('grp', 'dp'))  42.2 us
    convert_element_type x1, other arithmetic, on_device(): grad_scores = (attn_probs * (grad_probs - jnp.sum(attn_probs * grad_probs...  42.2 us
    dot_general x2, matrix products, on_device(): jnp.einsum('qhd,khd->hqk', context_grad_part, value_rows, preferred_eleme...  39.4 us
    dot_general x4, matrix products, contract_rows(): lax.dot_general(first_op, second_op, (((0,), (0,)), ((), ())), preferred_...  33.5 us
  transfers between devices with their start and end apart: 3, of which 2 were waited for; matrix products, arithmetic and copies ran while one was open for 7% of the time, Pallas kernels for 0%

commit v1 on v0

--- a/solution.py
+++ b/solution.py
@@ -16,6 +16,18 @@
 norm_eps = 1e-06
 neg_fill = -1e30
 decay_flags = (0.0, 0.0, 1.0, 0.0, 1.0, 0.0, 0.0, 0.0, 1.0, 0.0, 1.0, 0.0)
+
+
+def collect(array, axis, dim):
+    ways, here = (lax.axis_size(axis), lax.axis_index(axis))
+    grown, reach = (array, 1)
+    while reach < ways:
+        theirs = lax.ppermute(grown, axis, [(d, d ^ reach) for d in range(ways)])
+        mine_first = jnp.concatenate([grown, theirs], axis=dim)
+        theirs_first = jnp.concatenate([theirs, grown], axis=dim)
+        grown = jnp.where(here & reach == 0, mine_first, theirs_first)
+        reach = 2 * reach
+    return grown
 
 
 def layer_norm(values, gain, shift):
@@ -263,7 +275,7 @@
         / (jnp.sqrt(new_second / (1.0 - beta_two**step_count)) + adam_eps)
     )
     fresh_low = (current - learn_rate * (ratio + decay_rate * decay * current)).astype(jnp.bfloat16)
-    new_weights = lax.all_gather(fresh_low, "dp", axis=0, tiled=True)
+    new_weights = collect(fresh_low, "dp", 0)
     return (block_out, input_grad, summed, new_weights, new_first, new_second, summed_bias)
 
 

time: 1640 us -> 1840 us (1.12)
  waiting for transfers between devices: 950 us -> 1110 us
  other arithmetic: 106 us -> 163 us
  local copies, waits for them, and re-layouts: 272 us -> 253 us
    ppermute x0 -> x4, waiting for transfers between devices: none -> 438 us  [collect(): theirs = lax.ppermute(grown, axis, [(d, d ^ reach) for d in range(ways)])]
    all_gather x1 -> x0, waiting for transfers between devices: 283 us -> none  [on_device(): new_weights = lax.all_gather(fresh_low, 'dp', axis=0, tiled=True)]
    select_n x0 -> x4, other arithmetic: none -> 57 us  [collect(): grown = jnp.where(here & reach == 0, mine_first, theirs_first)]
    unnamed x215 -> x212, local copies, waits for them, and re-layouts: 188 us -> 169 us
    unnamed x4 -> x3, waiting for transfers between devices: 667 us -> 667 us
  transfers between devices with their start and end apart: 3 -> 6, of which waited for: 2 -> 5; matrix products, arithmetic and copies ran while one was open for 7% -> 6% of each run, Pallas kernels for 0% -> 0%
where the time goes in v1:
time: 1840 us; the launch traced here: 1820 us
  waiting for transfers between devices  1110 us (60%)
  local copies, waits for them, and re-layouts  253 us (14%)
  matrix products  237 us (13%)
  other arithmetic  163 us (9%)
  blocking collectives  42.4 us (2%)
    unnamed x3, waiting for transfers between devices  667 us
    ppermute x4, waiting for transfers between devices, collect(): theirs = lax.ppermute(grown, axis, [(d, d ^ reach) for d in range(ways)])  438 us
    unnamed x212, local copies, waits for them, and re-layouts  169 us
    select_n x4, other arithmetic, collect(): grown = jnp.where(here & reach == 0, mine_first, theirs_first)  57 us
    psum x1, blocking collectives, on_device(): totals = lax.psum(member * images, ('grp', 'dp'))  42.4 us
    convert_element_type x1, other arithmetic, on_device(): grad_scores = (attn_probs * (grad_probs - jnp.sum(attn_probs * grad_probs...  42 us
    dot_general x2, matrix products, on_device(): jnp.einsum('qhd,khd->hqk', context_grad_part, value_rows, preferred_eleme...  39.6 us
  transfers between devices with their start and end apart: 6, of which 5 were waited for; matrix products, arithmetic and copies ran while one was open for 6% of the time, Pallas kernels for 0%

profile of v1, /device:TPU:0, one launch (start us, length us, event | category | flops | bytes accessed | tf_op | source)
XLA Modules:
  0.0 1823.2 jit_solution(5088698939352009275)
XLA Ops:
  10.4 6.4 add_convert_fusion
  26.9 12.2 fusion.19
  39.1 11.8 fusion
  54.0 12.7 fusion.44
  69.0 12.2 fusion.20
  81.2 13.4 fusion.1
  97.1 8.5 fusion.45
  114.4 10.8 fusion.63
  125.3 16.5 convert_reduce_fusion
  141.7 7.3 fusion.73
  162.6 21.8 %multiply_reduce_fusion.1 = (f32[12,512]{1,0:T(8,128)S(1)}, f32[12,512,1024]{2,1,0:T(8,128)}) fusion(f32[12,512]{1,0:T(8,128)S(1)} %copy-done.43, f32[12,512,1024]{2,1,0:T(8,128)} %get-tuple-element.61, pred[512,1024]{1,0:T(8,128)(4,1)S(1)} %copy-done.18, bf16[512,12,64]{0,2,1:T(8,128)(2,1)S(1)} %bitcast.89, bf16[1024,12,64]{0,2,1:T(8,128)(2,1)S(1)} %bitcast.75), kind=kOutput, calls=%fused_computation.4 | convolution fusion | flops 836757504 | bytes 53264384 | tf_op jit(solution)/shard_map/qhd,khd->hqk/dot_general | solution.py:180
  184.5 17.7 multiply_reduce_fusion
  202.2 42.0 %multiply_convert_fusion = (bf16[12,512,1024]{2,1,0:T(8,128)(2,1)}, bf16[12,512,1024]{2,1,0:T(8,128)(2,1)}) fusion(f32[12,512,1024]{2,1,0:T(8,128)} %get-tuple-element.67, f32[12,512]{1,0:T(8,128)S(1)} %get-tuple-element.66, f32[12,512]{1,0:T(8,128)S(1)} %log_add_fusion, f32[12,512,1024]{2,1,0:T(8,128)} %get-tuple-element.59, ...), kind=kLoop, calls=%fused_computation | loop fusion | flops 75497472 | bytes 126976000 | tf_op jit(solution)/shard_map/convert_element_type | solution.py:185
  244.1 9.6 fusion.42
  253.8 8.8 fusion.74
  262.5 13.4 fusion.11
  276.5 6.3 fusion.43
  282.8 5.6 multiply_convert_fusion.3
  288.4 13.0 add_convert_fusion.2
  305.1 5.6 fusion.72
  311.9 42.4 %psum.14 = s32[3]{0:T(128)S(1)} all-reduce(s32[3]{0:T(128)S(1)} %fusion.51), channel_id=1, replica_groups=mesh['grp'=2,'dp'=16] {'grp','dp'}, use_global_device_ids=true, to_apply=%region_19.20 | all-reduce | flops 3 | bytes 24 | tf_op jit(solution)/shard_map/psum | solution.py:94
  357.0 9.0 convolution_multiply_fusion
  369.0 10.7 convolution_multiply_fusion.2
  379.8 10.9 convolution_multiply_fusion.1
  390.7 5.6 reshape.518
  407.6 10.7 reshape.520
  418.4 10.6 reshape.521
  429.0 5.6 fusion.32
  437.5 20.7 %dynamic-update-slice.24 = f32[16,442992]{1,0:T(8,128)} dynamic-update-slice(f32[16,442992]{1,0:T(8,128)} %dynamic-update-slice.23, f32[16,110592]{1,0:T(8,128)} %reshape.518, s32[]{} %constant.103, s32[]{} %constant.104) | dynamic-update-slice | bytes 14155780
  459.7 7.6 dynamic-update-slice.26
  471.7 6.5 constant_dynamic-update-slice_fusion
  479.6 27.0 %dynamic-update-slice.32 = f32[16,442992]{1,0:T(8,128)} dynamic-update-slice(f32[16,442992]{1,0:T(8,128)} %dynamic-update-slice.31, f32[16,147456]{1,0:T(8,128)} %reshape.521, s32[]{} %constant.103, s32[]{} %constant.111) | dynamic-update-slice | bytes 18874372
  533.6 8.7 dynamic-update-slice.1
  554.9 8.8 dynamic-update-slice.12
  576.0 667.0 %all-reduce.6.cloned.1.call-done = f32[16,442992]{1,0:T(8,128)} async-done(((f32[16,442992]{1,0:T(8,128)}), f32[16,442992]{1,0:T(8,128)}) %all-reduce.6.cloned.1.call-update) | async-done | bytes 28351504
  1243.0 7.5 constant_dynamic-slice_fusion.11
  1255.0 11.4 dynamic-update-slice.8
  1269.0 11.3 dynamic-update-slice.20
  1281.6 14.7 subtract_convert_fusion
  1297.8 39.0 %collective-permute-done = bf16[1,442992]{1,0:T(2,128)(2,1)} collective-permute-done((bf16[1,442992]{1,0:T(2,128)(2,1)S(1)}, bf16[1,442992]{1,0:T(2,128)(2,1)}, u32[]{:S(2)}, u32[]{:S(2)}) %collective-permute-start) | collective-permute-done | bytes 886016 | tf_op jit(solution)/shard_map/ppermute | solution.py:25
  1336.7 12.0 broadcast_select_fusion
  1350.3 38.1 %collective-permute-done.1 = bf16[2,442992]{1,0:T(2,128)(2,1)} collective-permute-done((bf16[2,442992]{1,0:T(2,128)(2,1)S(1)}, bf16[2,442992]{1,0:T(2,128)(2,1)}, u32[]{:S(2)}, u32[]{:S(2)}) %collective-permute-start.1) | collective-permute-done | bytes 1772000 | tf_op jit(solution)/shard_map/ppermute | solution.py:25
  1388.3 12.5 maximum_select_fusion.2
  1400.9 76.6 %collective-permute-done.2 = bf16[4,442992]{1,0:T(4,128)(2,1)} collective-permute-done((bf16[4,442992]{1,0:T(4,128)(2,1)S(1)}, bf16[4,442992]{1,0:T(4,128)(2,1)}, u32[]{:S(2)}, u32[]{:S(2)}) %collective-permute-start.2) | collective-permute-done | bytes 3543968 | tf_op jit(solution)/shard_map/ppermute | solution.py:25
  1477.5 13.1 maximum_select_fusion.1
  1495.0 12.0 add_convert_fusion.3
  1510.8 284.5 %collective-permute-done.3 = bf16[8,442992]{1,0:T(8,128)(2,1)} collective-permute-done((bf16[8,442992]{1,0:T(8,128)(2,1)}, bf16[8,442992]{1,0:T(8,128)(2,1)}, u32[]{:S(2)}, u32[]{:S(2)}) %collective-permute-start.3) | collective-permute-done | bytes 7087904 | tf_op jit(solution)/shard_map/ppermute | solution.py:25
  1795.3 19.4 %maximum_select_fusion = bf16[16,442992]{1,0:T(8,128)(2,1)} fusion(bf16[8,442992]{1,0:T(8,128)(2,1)} %collective-permute-done.3, bf16[8,442992]{1,0:T(8,128)(2,1)} %maximum_select_fusion.1, pred[]{:T(512)S(6)} %eq.71), kind=kLoop, calls=%fused_computation.18 | loop fusion | flops 63790848 | bytes 28351488 | tf_op jit(solution)/shard_map/jit(_where)/select_n | solution.py:28
  (319 shorter events, 146.1 us)
Async XLA Ops:
  7.2 1235.7 %all-reduce.6.cloned.1.call-start = ((), (), s32[]{:S(2)}) async-start(), calls=%async_computation.1 | async-start | bytes 56705024
  9.0 98.1 %copy-start.1 = (bf16[1024,768]{0,1:T(8,128)(2,1)}, bf16[1024,768]{0,1:T(8,128)(2,1)S(1)}, u32[]{:S(2)}) copy-start(bf16[1024,768]{0,1:T(8,128)(2,1)S(1)} %copy.76) | copy-start | bytes 4718596
  22.5 46.6 %copy-start.8 = (bf16[1024,768]{0,1:T(8,128)(2,1)}, bf16[1024,768]{0,1:T(8,128)(2,1)S(1)}, u32[]{:S(2)}) copy-start(bf16[1024,768]{0,1:T(8,128)(2,1)S(1)} %copy.80) | copy-start | bytes 4718596
  26.9 12.2 copy-start.17
  69.0 25.7 %copy-start.12 = (bf16[1024,768]{0,1:T(8,128)(2,1)S(1)}, bf16[1024,768]{0,1:T(8,128)(2,1)}, u32[]{:S(2)}) copy-start(bf16[1024,768]{0,1:T(8,128)(2,1)} %copy.77) | copy-start | bytes 4718596
  81.2 15.8 copy-start
  81.2 15.9 copy-start.19
  110.9 14.4 copy-start.41
  114.4 10.9 copy-start.60
  114.4 10.9 copy-start.14
  114.4 27.3 %slice-start.3 = ((s8[4718592]{0:T(1024)(128)(4,1)}), s8[4194304]{0:T(1024)(128)(4,1)S(1)}, s32[]{:S(2)}) async-start(s8[4718592]{0:T(1024)(128)(4,1)} %bitcast.71), calls=%async_computation.5 | async-start | bytes 8388608
  125.3 16.5 slice-start.4
  161.8 22.6 %copy-start.31 = (bf16[512,768]{0,1:T(8,128)(2,1)}, bf16[512,768]{0,1:T(8,128)(2,1)S(1)}, u32[]{:S(2)}) copy-start(bf16[512,768]{0,1:T(8,128)(2,1)S(1)} %get-tuple-element.52) | copy-start | bytes 2359300
  162.6 21.9 %copy-start.20 = (pred[512,1024]{1,0:T(8,128)(4,1)S(1)}, pred[512,1024]{1,0:T(8,128)(4,1)}, u32[]{:S(2)}) copy-start(pred[512,1024]{1,0:T(8,128)(4,1)} %get-tuple-element.55) | copy-start | bytes 1572868
  202.2 42.0 %copy-start.9 = (bf16[1024,768]{0,1:T(8,128)(2,1)S(1)}, bf16[1024,768]{0,1:T(8,128)(2,1)}, u32[]{:S(2)}) copy-start(bf16[1024,768]{0,1:T(8,128)(2,1)} %copy-done.8) | copy-start | bytes 4718596
  244.1 9.6 copy-start.24
  253.7 8.8 copy-start.32
  253.7 22.8 %slice-start = ((s8[12582912]{0:T(1024)(128)(4,1)}), s8[4194304]{0:T(1024)(128)(4,1)S(1)}, s32[]{:S(2)}) async-start(s8[12582912]{0:T(1024)(128)(4,1)} %bitcast.65), calls=%async_computation.2 | async-start | bytes 8388608
  253.7 22.8 %slice-start.1 = ((s8[12582912]{0:T(1024)(128)(4,1)}), s8[4194304]{0:T(1024)(128)(4,1)S(1)}, s32[]{:S(2)}) async-start(s8[12582912]{0:T(1024)(128)(4,1)} %bitcast.65), calls=%async_computation.3 | async-start | bytes 8388608
  262.5 13.4 copy-start.76
  262.5 14.0 slice-start.2
  288.4 13.1 copy-start.29
  288.4 13.1 copy-start.30
  301.7 9.0 copy-start.27
  305.1 50.5 %copy-start.77 = (s32[3]{0:T(128)S(1)}, s32[3]{0:T(128)}, u32[]{:S(2)}) copy-start(s32[3]{0:T(128)} %param.23) | copy-start | bytes 40
  305.1 51.9 %copy-start.2 = (bf16[1024,768]{0,1:T(8,128)(2,1)S(1)}, bf16[1024,768]{0,1:T(8,128)(2,1)}, u32[]{:S(2)}) copy-start(bf16[1024,768]{0,1:T(8,128)(2,1)} %copy-done.1) | copy-start | bytes 4718596
  305.1 51.9 %copy-start.45 = (f32[1024]{0:T(1024)S(1)}, f32[1024]{0:T(1024)}, u32[]{:S(2)}) copy-start(f32[1024]{0:T(1024)} %copy-done.44) | copy-start | bytes 12292
  305.1 51.9 %copy-start.47 = (f32[768]{0:T(1024)S(1)}, f32[768]{0:T(1024)}, u32[]{:S(2)}) copy-start(f32[768]{0:T(1024)} %copy-done.46) | copy-start | bytes 9220
  305.1 51.9 %copy-start.49 = (f32[1024]{0:T(1024)S(1)}, f32[1024]{0:T(1024)}, u32[]{:S(2)}) copy-start(f32[1024]{0:T(1024)} %copy-done.48) | copy-start | bytes 12292
  305.1 51.9 %copy-start.73 = (f32[768]{0:T(1024)S(1)}, f32[768]{0:T(1024)}, u32[]{:S(2)}) copy-start(f32[768]{0:T(1024)} %copy-done.72) | copy-start | bytes 9220
  357.0 9.0 copy-start.34
  357.0 9.0 copy-start.36
  366.1 13.7 slice-start.5
  368.9 10.8 copy-start.16
  369.0 10.8 slice-start.6
  369.0 10.8 slice-start.7
  369.0 10.8 copy-start.61
  407.6 10.7 copy-start.62
  418.4 10.7 copy-start.53
  437.5 22.2 %copy-start.23 = (f32[16,36864]{1,0:T(8,128)S(1)}, f32[16,36864]{1,0:T(8,128)}, u32[]{:S(2)}) copy-start(f32[16,36864]{1,0:T(8,128)} %reshape.519) | copy-start | bytes 7077892
  507.9 773.6 %all-reduce.4.cloned.1.call-start = ((), (), s32[]{:S(2)}) async-start(), calls=%async_computation | async-start | bytes 3544064 | tf_op jit(solution)/shard_map/psum | solution.py:236
  1242.9 10.2 copy-start.57
  1243.0 10.3 copy-start.71
  1296.3 40.4 %collective-permute-start = (bf16[1,442992]{1,0:T(2,128)(2,1)S(1)}, bf16[1,442992]{1,0:T(2,128)(2,1)}, u32[]{:S(2)}, u32[]{:S(2)}) collective-permute-start(bf16[1,442992]{1,0:T(2,128)(2,1)S(1)} %get-tuple-element.39), channel_id=1, source_target_pairs={{0,1},{1,0},{2,3},{3,2},{4,5},{5,4},{6,7},{7,6},{8,9},{9,8},{10,11... | collective-permute-start | bytes 2657960 | tf_op jit(solution)/shard_map/ppermute | solution.py:25
  1348.7 39.6 %collective-permute-start.1 = (bf16[2,442992]{1,0:T(2,128)(2,1)S(1)}, bf16[2,442992]{1,0:T(2,128)(2,1)}, u32[]{:S(2)}, u32[]{:S(2)}) collective-permute-start(bf16[2,442992]{1,0:T(2,128)(2,1)S(1)} %broadcast_select_fusion), channel_id=1, source_target_pairs={{0,2},{1,3},{2,0},{3,1},{4,6},{5,7},{6,4},{7,5},{8,10},{9,11},{10,... | collective-permute-start | bytes 5315912 | tf_op jit(solution)/shard_map/ppermute | solution.py:25
  1400.9 76.7 %collective-permute-start.2 = (bf16[4,442992]{1,0:T(4,128)(2,1)S(1)}, bf16[4,442992]{1,0:T(4,128)(2,1)}, u32[]{:S(2)}, u32[]{:S(2)}) collective-permute-start(bf16[4,442992]{1,0:T(4,128)(2,1)S(1)} %maximum_select_fusion.2), channel_id=1, source_target_pairs={{0,4},{1,5},{2,6},{3,7},{4,0},{5,1},{6,2},{7,3},{8,12},{9,13},{10,... | collective-permute-start | bytes 10631816 | tf_op jit(solution)/shard_map/ppermute | solution.py:25
  1490.6 304.6 %collective-permute-start.3 = (bf16[8,442992]{1,0:T(8,128)(2,1)}, bf16[8,442992]{1,0:T(8,128)(2,1)}, u32[]{:S(2)}, u32[]{:S(2)}) collective-permute-start(bf16[8,442992]{1,0:T(8,128)(2,1)} %maximum_select_fusion.1), channel_id=1, source_target_pairs={{0,8},{1,9},{2,10},{3,11},{4,12},{5,13},{6,14},{7,15},{8,0},{9,1},... | collective-permute-start | bytes 21263624 | tf_op jit(solution)/shard_map/ppermute | solution.py:25
  1510.8 303.9 %copy-start.25 = (f32[1,442992]{1,0:T(1,128)S(1)}, f32[1,442992]{1,0:T(1,128)}, u32[]{:S(2)}) copy-start(f32[1,442992]{1,0:T(1,128)} %all-reduce.4.cloned.1.call-done) | copy-start | bytes 5315908
  (45 other events, 148.9 us)
Sparse Core Ops, SparseCore 0:
  508.1 734.8 all-reduce.5
  1250.6 19.8 all-reduce.3
